TPU v7x, 32 devices: a whole 2x2x4 slice. The times are simulated.
32 devices in a mesh: groups: 2 (over y), ctx: 4 (over z), head: 4 (over x, core).
Axes of the slice: x: 2, y: 2, z: 4, core: 2. Of those that a mesh axis runs over, the one named last changes fastest.
Arguments:
- queries: bfloat16 [4096, 4096], P(('groups', 'ctx'), 'head'), parts along dimension 0, may hold values from -6 to 6
- key_rows: bfloat16 [4096, 4096], P(('groups', 'ctx'), 'head'), parts along dimension 0, may hold values from -6 to 6
- value_rows: bfloat16 [4096, 4096], P(('groups', 'ctx'), 'head'), parts along dimension 0, may hold values from -6 to 6
- norm_gain: float32 [4096], P('head'), may hold values from 0.1 to 1.9
- out_weight: bfloat16 [4096, 3072], P('head', 'ctx'), may hold values from -0.09375 to 0.09375
- out_grad: bfloat16 [4096, 3072], P(('groups', 'ctx'), 'head'), parts along dimension 0, may hold values from -6 to 6
Outputs:
- mixed: bfloat16 [4096, 3072], P(('groups', 'ctx'), 'head'), parts along dimension 0
- query_grad: bfloat16 [4096, 4096], P(('groups', 'ctx'), 'head'), parts along dimension 0
- key_grad: bfloat16 [4096, 4096], P(('groups', 'ctx'), 'head'), parts along dimension 0
- value_grad: bfloat16 [4096, 4096], P(('groups', 'ctx'), 'head'), parts along dimension 0
There are 2 independent parts, one for each index of `groups`. A program takes and returns all parts, laid end to end along the dimension named above; an argument that names none is the same for every part. Nothing has to cross between parts.
All inputs are finite; a program needn't handle non-finite values.
Results may differ from a plain program's by a relative error of at most 0.009.
Values may be sent and summed in bfloat16 or wider, within the bound.
A program may use at most 64 MiB of HBM per device.

v0:
```python
import jax
import jax.numpy as jnp
from jax import lax
from jax.sharding import PartitionSpec as P

HD = 128


def normed(attended, gain_grid):
    meansq = jnp.mean(attended * attended, axis=-1, keepdims=True)
    return attended * lax.rsqrt(meansq + 1e-06) * gain_grid


def on_device(queries, key_rows, value_rows, norm_gain, out_weight, out_grad):
    rows = queries.shape[0]
    heads_here = queries.shape[1] // HD
    query_loc = queries.reshape(rows, heads_here, HD)
    key_loc = key_rows.reshape(rows, heads_here, HD)
    value_loc = value_rows.reshape(rows, heads_here, HD)
    gain_grid = norm_gain.reshape(heads_here, HD)
    position = lax.axis_index("ctx")
    blocks = lax.axis_size("ctx")
    order = jnp.arange(blocks)
    causal = jnp.tril(jnp.ones((rows, rows), dtype=bool))
    states = jnp.einsum(
        "lhe,lhf->hef", key_loc, value_loc, preferred_element_type=jnp.float32
    ).astype(jnp.bfloat16)
    gathered = lax.all_gather(states[None], "ctx", axis=0, tiled=True)
    earlier_mask = order < position
    prefix = jnp.sum(
        jnp.where(earlier_mask[:, None, None, None], gathered.astype(jnp.float32), 0.0), axis=0
    )
    prefix_low = prefix.astype(jnp.bfloat16)
    raw_scores = jnp.einsum("lhe,mhe->hlm", query_loc, key_loc, preferred_element_type=jnp.float32)
    scores = jnp.where(causal, raw_scores, 0.0).astype(jnp.bfloat16)
    attended = jnp.einsum("lhe,hef->lhf", query_loc, prefix_low, preferred_element_type=jnp.float32)
    attended = attended + jnp.einsum(
        "hlm,mhf->lhf", scores, value_loc, preferred_element_type=jnp.float32
    )
    hidden = normed(attended, gain_grid).astype(jnp.bfloat16).reshape(rows, heads_here * HD)
    full_weight = lax.all_gather(out_weight, "ctx", axis=1, tiled=True)
    partial_value = jnp.dot(hidden, full_weight, preferred_element_type=jnp.float32)
    mixed = lax.psum_scatter(
        partial_value.astype(jnp.bfloat16), "head", scatter_dimension=1, tiled=True
    )
    grad_cols = lax.all_gather(out_grad, "head", axis=1, tiled=True)
    grad_hidden = lax.dot_general(
        grad_cols, full_weight, (((1,), (1,)), ((), ())), preferred_element_type=jnp.float32
    )
    grad_hidden = grad_hidden.reshape(rows, heads_here, HD)
    _, pullback = jax.vjp(lambda values_in: normed(values_in, gain_grid), attended)
    grad_attended = pullback(grad_hidden)[0].astype(jnp.bfloat16)
    grad_state = jnp.einsum(
        "lhe,lhf->hef", query_loc, grad_attended, preferred_element_type=jnp.float32
    ).astype(jnp.bfloat16)
    gathered_grads = lax.all_gather(grad_state[None], "ctx", axis=0, tiled=True)
    later_mask = order > position
    suffix = jnp.sum(
        jnp.where(later_mask[:, None, None, None], gathered_grads.astype(jnp.float32), 0.0), axis=0
    )
    suffix_low = suffix.astype(jnp.bfloat16)
    raw_grad = jnp.einsum(
        "lhf,mhf->hlm", grad_attended, value_loc, preferred_element_type=jnp.float32
    )
    grad_scores = jnp.where(causal, raw_grad, 0.0).astype(jnp.bfloat16)
    query_grad = jnp.einsum(
        "hlm,mhe->lhe", grad_scores, key_loc, preferred_element_type=jnp.float32
    )
    query_grad = query_grad + jnp.einsum(
        "lhf,hef->lhe", grad_attended, prefix_low, preferred_element_type=jnp.float32
    )
    key_grad = jnp.einsum(
        "hlm,lhe->mhe", grad_scores, query_loc, preferred_element_type=jnp.float32
    )
    key_grad = key_grad + jnp.einsum(
        "mhf,hef->mhe", value_loc, suffix_low, preferred_element_type=jnp.float32
    )
    value_grad = jnp.einsum(
        "hlm,lhf->mhf", scores, grad_attended, preferred_element_type=jnp.float32
    )
    value_grad = value_grad + jnp.einsum(
        "mhe,hef->mhf", key_loc, suffix_low, preferred_element_type=jnp.float32
    )
    flat = (rows, heads_here * HD)
    return (
        mixed,
        query_grad.reshape(flat).astype(jnp.bfloat16),
        key_grad.reshape(flat).astype(jnp.bfloat16),
        value_grad.reshape(flat).astype(jnp.bfloat16),
    )


def solution(mesh):
    placed = (
        P(("groups", "ctx"), "head"),
        P(("groups", "ctx"), "head"),
        P(("groups", "ctx"), "head"),
        P("head"),
        P("head", "ctx"),
        P(("groups", "ctx"), "head"),
    )
    return jax.shard_map(
        on_device,
        mesh=mesh,
        in_specs=placed,
        out_specs=(
            P(("groups", "ctx"), "head"),
            P(("groups", "ctx"), "head"),
            P(("groups", "ctx"), "head"),
            P(("groups", "ctx"), "head"),
        ),
        check_vma=False,
    )
```

profile of v0, /device:TPU:0, one launch (start us, length us, event | category | flops | bytes accessed | tf_op | source)
XLA Modules:
  0.0 275.1 jit_solution(6222137651806970024)
XLA Ops:
  7.2 0.0 copy-start
  7.2 0.0 all-gather.11.cloned.1.call-start
  7.2 1.6 copy.60
  8.8 0.7 copy.31
  9.5 0.0 copy-start.5
  9.5 1.0 copy-done.5
  10.5 1.2 convolution_convert_fusion.2
  11.6 0.0 all-gather.11.cloned.1.call-update
  11.7 0.0 all-gather.9.cloned.1.call-start
  11.7 0.7 all-gather.9.cloned.1.call-update
  12.4 0.0 all-gather.7.cloned.1.call-start
  12.4 0.7 all-gather.7.cloned.1.call-update
  13.1 0.0 all-gather.13.cloned.1.call-start
  13.2 0.1 iota_compare_fusion
  13.3 0.7 copy-done.10
  14.0 3.3 %select_convert_fusion.1 = bf16[8,512,512]{2,1,0:T(8,128)(2,1)} fusion(pred[512,512]{1,0:T(8,128)(4,1)S(1)} %iota_compare_fusion, bf16[512,1024]{1,0:T(8,128)(2,1)S(1)} %copy-done.3, bf16[512,1024]{1,0:T(8,128)(2,1)S(1)} %copy-done.7), kind=kOutput, calls=%fused_computation.1 | convolution fusion | flops 541065216 | bytes 6553600 | tf_op jit(solution)/shard_map/lhe,mhe->hlm/dot_general | solution.py:34
  17.3 25.1 %all-gather.11.cloned.1.call-done = bf16[32,128,128]{2,1,0:T(8,128)(2,1)} async-done(((bf16[8,128,128]{2,1,0:T(8,128)(2,1)}), bf16[32,128,128]{2,1,0:T(8,128)(2,1)}) %all-gather.11.cloned.1.call-update) | async-done | bytes 1048592 | tf_op jit(solution)/shard_map/all_gather | solution.py:28
  42.4 1.5 fusion.2
  43.9 1.7 fusion.10
  45.7 0.0 copy-start.12
  45.7 26.4 %all-gather.9.cloned.1.call-done = bf16[512,3072]{1,0:T(8,128)(2,1)} async-done(((bf16[512,768]{1,0:T(8,128)(2,1)}), bf16[512,3072]{1,0:T(8,128)(2,1)}) %all-gather.9.cloned.1.call-update) | async-done | bytes 3145744 | tf_op jit(solution)/shard_map/all_gather | solution.py:46
  72.1 117.0 %all-gather.7.cloned.1.call-done = bf16[1024,3072]{1,0:T(8,128)(2,1)} async-done(((bf16[1024,768]{1,0:T(8,128)(2,1)}), bf16[1024,3072]{1,0:T(8,128)(2,1)}) %all-gather.7.cloned.1.call-update) | async-done | bytes 6291472 | tf_op jit(solution)/shard_map/all_gather | solution.py:41
  189.0 6.7 %fusion.33 = f32[512,1024]{0,1:T(8,128)S(1)} fusion(bf16[512,3072]{1,0:T(8,128)(2,1)} %all-gather.9.cloned.1.call-done, bf16[1024,3072]{1,0:T(8,128)(2,1)} %all-gather.7.cloned.1.call-done), kind=kOutput, calls=%fused_computation.53 | convolution fusion | flops 3221225472 | bytes 11534336 | tf_op jit(solution)/shard_map/dot_general | solution.py:47
  195.7 1.8 multiply_reduce_fusion
  197.6 0.7 fusion
  198.3 0.5 copy-done.8
  198.8 1.2 fusion.5
  200.0 1.8 copy.45
  201.8 0.0 all-gather.13.cloned.1.call-update
  201.8 0.2 reduce-scatter.2.cloned.1.call-start
  202.0 7.7 %convolution_convert_fusion = bf16[512,3072]{1,0:T(8,128)(2,1)} fusion(bf16[512,1024]{0,1:T(8,128)(2,1)S(1)} %bitcast.117, bf16[1024,3072]{1,0:T(8,128)(2,1)} %all-gather.7.cloned.1.call-done), kind=kOutput, calls=%fused_computation.2 | convolution fusion | flops 3222798336 | bytes 10485760 | tf_op jit(solution)/shard_map/dot_general | solution.py:42
  209.8 0.0 reduce-scatter.2.cloned.1.call-update
  209.8 0.9 copy-done.11
  210.7 1.4 select_convert_fusion
  212.1 1.5 fusion.34
  213.6 0.5 copy-done.2
  214.1 0.4 fusion.4
  214.5 1.3 copy.49
  215.9 4.4 %fusion.35 = f32[8,128,512]{2,1,0:T(8,128)} fusion(bf16[512,8,128]{0,2,1:T(8,128)(2,1)S(1)} %get-tuple-element.14, bf16[8,512,512]{2,1,0:T(8,128)(2,1)} %select_convert_fusion.1), kind=kOutput, calls=%fused_computation.55 | convolution fusion | flops 536870912 | bytes 7340032 | tf_op jit(solution)/shard_map/hlm,lhf->mhf/dot_general | solution.py:78
  220.2 7.8 %all-gather.13.cloned.1.call-done = bf16[32,128,128]{2,1,0:T(8,128)(2,1)} async-done(((bf16[8,128,128]{2,1,0:T(8,128)(2,1)}), bf16[32,128,128]{2,1,0:T(8,128)(2,1)}) %all-gather.13.cloned.1.call-update) | async-done | bytes 1048592 | tf_op jit(solution)/shard_map/all_gather | solution.py:56
  228.1 1.5 fusion.1
  229.6 2.1 add_convert_fusion
  231.7 1.3 copy.51
  233.0 0.4 fusion.14
  233.5 0.8 copy-done.9
  234.2 3.6 %fusion.3 = bf16[512,8,128]{0,2,1:T(8,128)(2,1)S(1)} fusion(f32[8,128,512]{2,1,0:T(8,128)S(1)} %fusion.14, bf16[8,512,512]{2,1,0:T(8,128)(2,1)} %copy-done.2, bf16[512,1024]{1,0:T(8,128)(2,1)S(1)} %copy-done.9), kind=kOutput, calls=%fused_computation.10 | convolution fusion | flops 537919488 | bytes 8388608 | tf_op jit(solution)/shard_map/hlm,lhe->mhe/dot_general | solution.py:72
  237.8 1.3 copy.50
  239.2 29.4 %reduce-scatter.2.cloned.1.call-done = bf16[512,768]{1,0:T(8,128)(2,1)} async-done(((bf16[512,3072]{1,0:T(8,128)(2,1)}), bf16[512,768]{1,0:T(8,128)(2,1)}) %reduce-scatter.2.cloned.1.call-update) | async-done | bytes 786448 | tf_op jit(solution)/shard_map/reduce_scatter | solution.py:43
  (20 shorter events, 0.1 us)
Async XLA Ops:
  7.2 3.3 %copy-start = (bf16[512,1024]{1,0:T(8,128)(2,1)S(1)}, bf16[512,1024]{1,0:T(8,128)(2,1)}, u32[]{:S(2)}) copy-start(bf16[512,1024]{1,0:T(8,128)(2,1)} %param.8) | copy-start | bytes 3145732
  7.2 35.3 %all-gather.11.cloned.1.call-start = ((), (), s32[]{:S(2)}) async-start(), calls=%async_computation.4 | async-start | bytes 1310720 | tf_op jit(solution)/shard_map/all_gather | solution.py:28
  9.5 1.0 copy-start.5
  11.6 2.4 copy-start.3
  11.6 2.4 copy-start.7
  11.7 60.4 %all-gather.9.cloned.1.call-start = ((), (), s32[]{:S(2)}) async-start(), calls=%async_computation.3 | async-start | bytes 3932160 | tf_op jit(solution)/shard_map/all_gather | solution.py:46
  12.4 176.6 %all-gather.7.cloned.1.call-start = ((), (), s32[]{:S(2)}) async-start(), calls=%async_computation.1 | async-start | bytes 7864320 | tf_op jit(solution)/shard_map/all_gather | solution.py:41
  13.1 214.9 %all-gather.13.cloned.1.call-start = ((), (), s32[]{:S(2)}) async-start(), calls=%async_computation.5 | async-start | bytes 1310720 | tf_op jit(solution)/shard_map/all_gather | solution.py:56
  13.3 0.7 copy-start.10
  45.7 150.0 %copy-start.12 = (f32[1024]{0:T(1024)S(1)}, f32[1024]{0:T(1024)}, u32[]{:S(2)}) copy-start(f32[1024]{0:T(1024)} %param.9) | copy-start | bytes 12292
  189.0 6.7 %copy-start.1 = (bf16[8,512,512]{2,1,0:T(8,128)(2,1)S(1)}, bf16[8,512,512]{2,1,0:T(8,128)(2,1)}, u32[]{:S(2)}) copy-start(bf16[8,512,512]{2,1,0:T(8,128)(2,1)} %select_convert_fusion.1) | copy-start | bytes 12582916
  197.6 1.2 copy-start.8
  201.8 66.7 %reduce-scatter.2.cloned.1.call-start = ((), (), s32[]{:S(2)}) async-start(), calls=%async_computation.2 | async-start | bytes 3932160 | tf_op jit(solution)/shard_map/reduce_scatter | solution.py:43
  209.8 0.9 copy-start.11
  210.7 1.4 copy-start.6
  212.1 2.0 copy-start.2
  215.9 13.7 %copy-start.4 = (bf16[512,1024]{1,0:T(8,128)(2,1)S(1)}, bf16[512,1024]{1,0:T(8,128)(2,1)}, u32[]{:S(2)}) copy-start(bf16[512,1024]{1,0:T(8,128)(2,1)} %param.7) | copy-start | bytes 3145732
  233.0 1.2 copy-start.9
Sparse Core Ops, SparseCore 0:
  11.8 30.6 all-gather.10
  44.0 28.0 all-gather.8
  73.6 115.3 all-gather.6
  201.9 26.1 all-gather.12
  231.0 37.4 reduce-scatter.1
where the time goes:
time: 276 us; the launch traced here: 275 us
  waiting for transfers between devices  207 us (75%)
  matrix products  37.4 us (14%)
  between operations  14 us (5%)
  local copies, waits for them, and re-layouts  12.4 us (4%)
  other arithmetic  3.79 us (1%)
    all_gather x1, waiting for transfers between devices, on_device(): full_weight = lax.all_gather(out_weight, 'ctx', axis=1, tiled=True)  117 us
    reduce_scatter x1, waiting for transfers between devices, on_device(): lax.psum_scatter(partial_value.astype(jnp.bfloat16), 'head', scatter_dime...  29.4 us
    all_gather x1, waiting for transfers between devices, on_device(): grad_cols = lax.all_gather(out_grad, 'head', axis=1, tiled=True)  26.4 us
    all_gather x1, waiting for transfers between devices, on_device(): gathered = lax.all_gather(states[None], 'ctx', axis=0, tiled=True)  25.1 us
    unnamed x30, local copies, waits for them, and re-layouts  9.9 us
    all_gather x1, waiting for transfers between devices, on_device(): gathered_grads = lax.all_gather(grad_state[None], 'ctx', axis=0, tiled=True)  7.84 us
    dot_general x1, matrix products, on_device(): jnp.dot(hidden, full_weight, preferred_element_type=jnp.float32)  7.73 us
    dot_general x1, matrix products, on_device(): lax.dot_general(grad_cols, full_weight, (((1,), (1,)), ((), ())), preferr...  6.66 us
  transfers between devices with their start and end apart: 5, of which 5 were waited for; matrix products, arithmetic and copies ran while one was open for 12% of the time, Pallas kernels for 0%

commit v1 on v0

--- a/solution.py
+++ b/solution.py
@@ -1,6 +1,8 @@
 import jax
 import jax.numpy as jnp
 from jax import lax
+from jax.experimental import pallas as pl
+from jax.experimental.pallas import tpu as pltpu
 from jax.sharding import PartitionSpec as P
 
 HD = 128
@@ -90,6 +92,358 @@
     )
 
 
+MESH_OF_KERNEL = {"groups": 2, "ctx": 4, "head": 4}
+PIECES = 3
+SPANS = 4
+F32 = jnp.float32
+BF16 = jnp.bfloat16
+NN = (((1,), (0,)), ((), ()))
+NT = (((1,), (1,)), ((), ()))
+TN = (((0,), (0,)), ((), ()))
+
+
+def mul(a, b, dims):
+    return lax.dot_general(a, b, dims, preferred_element_type=F32)
+
+
+def fused_kernel(
+    q_ref, k_ref, v_ref, gain_ref, w_ref, og_ref,
+    mixed_ref, dq_ref, dk_ref, dv_ref,
+    wall, ogall, att, gh, scores, hid, dout,
+    pacc, csend, cin, xsend, xin, sbuf, pbuf, psend, rbuf, gbuf, gsend,
+    local_sem, up_sem, down_sem, z_sem, ysend_sem, yrecv_sem, ogsend_sem, ogrecv_sem,
+    psend_sem, precv_sem, rsend_sem, rrecv_sem, csend_sem, crecv_sem, xsend_sem, xrecv_sem,
+):
+    rows = q_ref.shape[0]
+    heads = q_ref.shape[1] // HD
+    half_cols = wall.shape[3]
+    piece = half_cols // PIECES
+    part = heads // SPANS
+    g = lax.axis_index("groups")
+    z = lax.axis_index("ctx")
+    h = lax.axis_index("head")
+    last = 3
+    x, c = h // 2, h % 2
+    to_up, to_down = {"ctx": z + 1}, {"ctx": z - 1}
+    to_y = {"groups": 1 - g}
+    to_core = {"head": x * 2 + 1 - c}
+    to_x = {"head": (1 - x) * 2 + c}
+
+    def remote(src, dst, send, recv, to):
+        return pltpu.make_async_remote_copy(
+            src_ref=src, dst_ref=dst, send_sem=send, recv_sem=recv,
+            device_id=to, device_id_type=pl.DeviceIdType.MESH,
+        )
+
+    barrier = pltpu.get_barrier_semaphore()
+
+    def greet(to):
+        pl.semaphore_signal(barrier, inc=1, device_id=to, device_id_type=pl.DeviceIdType.MESH)
+
+    greet(to_y)
+    greet(to_core)
+    greet(to_x)
+    pl.when(z < last)(lambda: greet(to_up))
+    pl.when(z > 0)(lambda: greet(to_down))
+    pl.semaphore_wait(barrier, 3 + jnp.where(z < last, 1, 0) + jnp.where(z > 0, 1, 0))
+
+    def cols(index, width):
+        return pl.ds(pl.multiple_of(index * width, HD), width)
+
+    def head_cols(index):
+        return cols(index, HD)
+
+    def w_piece(k, half, j):
+        return wall.at[k, half, :, cols(j, piece)]
+
+    def own_piece(j):
+        return w_ref.at[:, cols(g * PIECES + j, piece)]
+
+    def z_copy(src, k, j, send, to):
+        return remote(src, w_piece(k, g, j), send.at[k, j], z_sem.at[k, j], to)
+
+    def up_copy(k, j, src=None):
+        return z_copy(w_piece(k, g, j) if src is None else src, k, j, up_sem, to_up)
+
+    def down_copy(k, j, src=None):
+        return z_copy(w_piece(k, g, j) if src is None else src, k, j, down_sem, to_down)
+
+    def y_copy(k, half, j):
+        return remote(w_piece(k, half, j), w_piece(k, half, j), ysend_sem.at[k, j], yrecv_sem.at[k, j], to_y)
+
+    def og_copy(slot, index, src, to):
+        return remote(src, ogall.at[slot], ogsend_sem.at[index], ogrecv_sem.at[index], to)
+
+    og_core = og_copy(h, 0, og_ref, to_core)
+    og_x = og_copy(h, 1, og_ref, to_x)
+    across = (1 - x) * 2 + c
+    og_forward = og_copy(across, 2, ogall.at[across], to_core)
+    own_og = pltpu.make_async_copy(og_ref, ogall.at[h], local_sem.at[2])
+    own_w = [
+        pltpu.make_async_copy(w_ref.at[:, i * half_cols:(i + 1) * half_cols], wall.at[z, i], local_sem.at[i])
+        for i in range(2)
+    ]
+
+    for j in range(PIECES):
+        pl.when(z < last)(lambda j=j: up_copy(z, j, own_piece(j)).start())
+        pl.when(z > 0)(lambda j=j: down_copy(z, j, own_piece(j)).start())
+    og_x.start()
+    og_core.start()
+    own_og.start()
+    for copy in own_w:
+        copy.start()
+
+    def span(ref, i):
+        return ref.at[pl.ds(i * part, part)]
+
+    def p_copy(i, src):
+        return remote(span(src, i), span(pbuf, i), psend_sem.at[i], precv_sem.at[i], to_up)
+
+    def r_copy(i, src):
+        return remote(span(src, i), span(gbuf, i), rsend_sem.at[i], rrecv_sem.at[i], to_down)
+
+    def state_step(i, carry):
+        sbuf[i] = mul(k_ref[:, head_cols(i)], v_ref[:, head_cols(i)], TN).astype(BF16)
+        return carry
+
+    lax.fori_loop(0, heads, state_step, 0)
+
+    @pl.when(z == 0)
+    def _():
+        for i in range(SPANS):
+            p_copy(i, sbuf).start()
+        pbuf[...] = jnp.zeros_like(pbuf)
+
+    causal = lax.broadcasted_iota(jnp.int32, (rows, rows), 0) >= lax.broadcasted_iota(jnp.int32, (rows, rows), 1)
+
+    def score_step(i, carry):
+        own = jnp.where(causal, mul(q_ref[:, head_cols(i)], k_ref[:, head_cols(i)], NT), 0.0).astype(BF16)
+        scores[i] = own
+        att[:, head_cols(i)] = mul(own, v_ref[:, head_cols(i)], NN)
+        return carry
+
+    lax.fori_loop(0, heads, score_step, 0)
+
+    def pass_on(s):
+        for j in range(PIECES):
+            @pl.when((s > 0) & (z - s >= 0))
+            def _():
+                k = z - s
+                up_copy(k, j).wait_recv()
+                y_copy(k, g, j).start()
+                pl.when(z < last)(lambda: up_copy(k, j).start())
+
+            @pl.when((s > 0) & (z + s <= last))
+            def _():
+                k = z + s
+                down_copy(k, j).wait_recv()
+                y_copy(k, g, j).start()
+                pl.when(z > 0)(lambda: down_copy(k, j).start())
+
+    og_copy(across, 1, og_ref, to_x).wait_recv()
+    og_forward.start()
+    pass_on(1)
+
+    @pl.when(z > 0)
+    def _():
+        for i in range(SPANS):
+            p_copy(i, psend).wait_recv()
+
+            @pl.when(z < last)
+            def _():
+                at = pl.ds(i * part, part)
+                psend[at] = (sbuf[at].astype(F32) + pbuf[at].astype(F32)).astype(BF16)
+                p_copy(i, psend).start()
+
+    def hidden_step(i, carry):
+        at = head_cols(i)
+        whole = att[:, at] + mul(q_ref[:, at], pbuf[i], NN)
+        att[:, at] = whole
+        scale = lax.rsqrt(jnp.mean(whole * whole, axis=-1, keepdims=True) + 1e-06)
+        hid[:, at] = (whole * scale * gain_ref[:, at]).astype(BF16)
+        return carry
+
+    lax.fori_loop(0, heads, hidden_step, 0)
+
+    own_og.wait()
+    for copy in own_w:
+        copy.wait()
+    og_core.wait_recv()
+    og_forward.wait_recv()
+    gh[...] = jnp.zeros_like(gh)
+
+    def core_copy(xk, half):
+        return remote(csend.at[xk, half], cin.at[xk, half], csend_sem.at[xk, half], crecv_sem.at[xk, half], to_core)
+
+    def x_copy(half):
+        return remote(xsend.at[half], xin.at[half], xsend_sem.at[half], xrecv_sem.at[half], to_x)
+
+    def work(k, half):
+        xk, ck = k // 2, k % 2
+        weight = wall[k, half]
+        term = mul(hid[...], weight, NN)
+
+        @pl.when(ck != c)
+        def _():
+            csend[xk, half] = term.astype(BF16)
+            core_copy(xk, half).start()
+
+        @pl.when(ck == c)
+        def _():
+            pacc[xk, half] = term
+
+        gh[...] += mul(ogall[k, :, cols(half, half_cols)], weight, NT)
+
+        @pl.when(ck == c)
+        def _():
+            core_copy(xk, half).wait_recv()
+            both = pacc[xk, half] + cin[xk, half].astype(F32)
+
+            @pl.when(xk == x)
+            def _():
+                pacc[xk, half] = both
+
+            @pl.when(xk != x)
+            def _():
+                xsend[half] = both.astype(BF16)
+                x_copy(half).start()
+
+    def ring_step(s, carry):
+        pl.when(s > 1)(lambda: pass_on(s))
+
+        def sub_step(i, inner):
+            above, late = i % 2, i // 2
+            k = jnp.where(above == 0, z - s, z + s)
+            half = jnp.where(late == 0, g, 1 - g)
+
+            @pl.when((k >= 0) & (k <= last) & ((s > 0) | (above == 0)))
+            def _():
+                @pl.when((late == 1) & (s > 0))
+                def _():
+                    for j in range(PIECES):
+                        y_copy(k, half, j).wait_recv()
+                work(k, half)
+            return inner
+
+        lax.fori_loop(0, 4, sub_step, 0)
+        return carry
+
+    lax.fori_loop(0, 4, ring_step, 0)
+
+    def norm_step(i, carry):
+        at = head_cols(i)
+        whole = att[:, at]
+        scale = lax.rsqrt(jnp.mean(whole * whole, axis=-1, keepdims=True) + 1e-06)
+        scaled = gh[:, at] * gain_ref[:, at]
+        inner = jnp.mean(scaled * whole, axis=-1, keepdims=True) * scale * scale
+        grad = ((scaled - whole * inner) * scale).astype(BF16)
+        dout[:, at] = grad
+        rbuf[i] = mul(q_ref[:, at], grad, TN).astype(BF16)
+        return carry
+
+    lax.fori_loop(0, heads, norm_step, 0)
+
+    @pl.when(z == last)
+    def _():
+        for i in range(SPANS):
+            r_copy(i, rbuf).start()
+        gbuf[...] = jnp.zeros_like(gbuf)
+
+    def grad_step(i, carry):
+        at = head_cols(i)
+        grad = dout[:, at]
+        back = jnp.where(causal, mul(grad, v_ref[:, at], NT), 0.0).astype(BF16)
+        dq_ref[:, at] = (mul(back, k_ref[:, at], NN) + mul(grad, pbuf[i], NT)).astype(BF16)
+        att[:, at] = mul(back, q_ref[:, at], TN)
+        gh[:, at] = mul(scores[i], grad, TN)
+        return carry
+
+    lax.fori_loop(0, heads, grad_step, 0)
+
+    @pl.when(z < last)
+    def _():
+        for i in range(SPANS):
+            r_copy(i, gsend).wait_recv()
+
+            @pl.when(z > 0)
+            def _():
+                at = pl.ds(i * part, part)
+                gsend[at] = (rbuf[at].astype(F32) + gbuf[at].astype(F32)).astype(BF16)
+                r_copy(i, gsend).start()
+
+    def last_step(i, carry):
+        at = head_cols(i)
+        dk_ref[:, at] = (att[:, at] + mul(v_ref[:, at], gbuf[i], NT)).astype(BF16)
+        dv_ref[:, at] = (gh[:, at] + mul(k_ref[:, at], gbuf[i], NN)).astype(BF16)
+        return carry
+
+    lax.fori_loop(0, heads, last_step, 0)
+
+    for half in range(2):
+        x_copy(half).wait_recv()
+        mixed_ref[:, half * half_cols:(half + 1) * half_cols] = (
+            pacc[x, half] + xin[half].astype(F32)
+        ).astype(BF16)
+
+    og_core.wait_send()
+    og_x.wait_send()
+    og_forward.wait_send()
+    for half in range(2):
+        x_copy(half).wait_send()
+        for xk in range(2):
+            core_copy(xk, half).wait_send()
+    for i in range(SPANS):
+        pl.when(z < last)(lambda i=i: p_copy(i, sbuf).wait_send())
+        pl.when(z > 0)(lambda i=i: r_copy(i, rbuf).wait_send())
+    for k in range(4):
+        for j in range(PIECES):
+            pl.when((z >= k) & (z < last))(lambda k=k, j=j: up_copy(k, j).wait_send())
+            pl.when((z <= k) & (z > 0))(lambda k=k, j=j: down_copy(k, j).wait_send())
+            pl.when(z != k)(lambda k=k, j=j: y_copy(k, g, j).wait_send())
+
+
+def on_device_fused(queries, key_rows, value_rows, norm_gain, out_weight, out_grad):
+    rows, width = queries.shape
+    heads = width // HD
+    share = out_weight.shape[1]
+    half = share // 2
+    inside = pl.BlockSpec(memory_space=pltpu.VMEM)
+    anywhere = pl.BlockSpec(memory_space=pl.ANY)
+    grid_of = jax.ShapeDtypeStruct((rows, width), BF16)
+    dma = pltpu.SemaphoreType.DMA
+    states = pltpu.VMEM((heads, HD, HD), BF16)
+    return pl.pallas_call(
+        fused_kernel,
+        out_shape=(jax.ShapeDtypeStruct((rows, share), BF16), grid_of, grid_of, grid_of),
+        in_specs=[inside] * 4 + [anywhere] * 2,
+        out_specs=(inside,) * 4,
+        scratch_shapes=[
+            pltpu.VMEM((4, 2, width, half), BF16),
+            pltpu.VMEM((4, rows, share), BF16),
+            pltpu.VMEM((rows, width), F32),
+            pltpu.VMEM((rows, width), F32),
+            pltpu.VMEM((heads, rows, rows), BF16),
+            pltpu.VMEM((rows, width), BF16),
+            pltpu.VMEM((rows, width), BF16),
+            pltpu.VMEM((2, 2, rows, half), F32),
+            pltpu.VMEM((2, 2, rows, half), BF16),
+            pltpu.VMEM((2, 2, rows, half), BF16),
+            pltpu.VMEM((2, rows, half), BF16),
+            pltpu.VMEM((2, rows, half), BF16),
+            states, states, states, states, states, states,
+            dma((3,)),
+            dma((4, PIECES)), dma((4, PIECES)), dma((4, PIECES)), dma((4, PIECES)), dma((4, PIECES)),
+            dma((3,)), dma((3,)),
+            dma((SPANS,)), dma((SPANS,)), dma((SPANS,)), dma((SPANS,)),
+            dma((2, 2)), dma((2, 2)), dma((2,)), dma((2,)),
+        ],
+        compiler_params=pltpu.CompilerParams(
+            collective_id=0, has_side_effects=True, vmem_limit_bytes=56 * 1024 * 1024
+        ),
+        cost_estimate=pl.CostEstimate(flops=12 * 10**9, bytes_accessed=10**7, transcendentals=rows * heads),
+    )(queries, key_rows, value_rows, norm_gain.reshape(1, width), out_weight, out_grad)
+
+
 def solution(mesh):
     placed = (
         P(("groups", "ctx"), "head"),
@@ -99,8 +453,9 @@
         P("head", "ctx"),
         P(("groups", "ctx"), "head"),
     )
+    fused = all(mesh.shape[name] == size for name, size in MESH_OF_KERNEL.items())
     return jax.shard_map(
-        on_device,
+        on_device_fused if fused else on_device,
         mesh=mesh,
         in_specs=placed,
         out_specs=(

time: 276 us -> 131 us (0.47)
  waiting for transfers between devices: 207 us -> 0 us
  Pallas kernels: 0 us -> 125 us
  matrix products: 37.4 us -> 0 us
  between operations: 14 us -> 0.66 us
  local copies, waits for them, and re-layouts: 12.4 us -> 5.76 us
  other arithmetic: 3.79 us -> 0 us
    all_gather x4 -> x0, waiting for transfers between devices: 176 us -> none  [the longest x1 117 us: on_device(): full_weight = lax.all_gather(out_weight, 'ctx', axis=1, tiled=True)]
    pallas_call x0 -> x1, Pallas kernels: none -> 125 us  [on_device_fused(): pl.pallas_call(fused_kernel, out_shape=(jax.ShapeDtypeStruct((rows, share...]
    dot_general x14 -> x0, matrix products: 37.4 us -> none  [the longest x1 7.73 us: on_device(): jnp.dot(hidden, full_weight, preferred_element_type=jnp.float32)]
    reduce_scatter x1 -> x0, waiting for transfers between devices: 29.4 us -> none  [on_device(): lax.psum_scatter(partial_value.astype(jnp.bfloat16), 'head', scatter_dime...]
    unnamed x30 -> x10, local copies, waits for them, and re-layouts: 9.9 us -> 5.76 us
    reduce_sum x2 -> x0, other arithmetic: 2.99 us -> none  [the longest x1 1.5 us: on_device(): jnp.sum(jnp.where(earlier_mask[:, None, None, None], gathered.astype(jnp....]
  transfers between devices with their start and end apart: 5 -> 0, of which waited for: 5 -> 0; matrix products, arithmetic and copies ran while one was open for 12% -> 0% of each run, Pallas kernels for 0% -> 0%
where the time goes in v1:
time: 131 us
  Pallas kernels  125 us (95%)
  local copies, waits for them, and re-layouts  5.76 us (4%)
    pallas_call x1, Pallas kernels, on_device_fused(): pl.pallas_call(fused_kernel, out_shape=(jax.ShapeDtypeStruct((rows, share...  125 us
    unnamed x10, local copies, waits for them, and re-layouts  5.76 us

profile of v1, /device:TPU:0, one launch (start us, length us, event | category | flops | bytes accessed | tf_op | source)
XLA Modules:
  0.0 131.2 jit_solution(10057827770665430110)
XLA Ops:
  0.6 124.8 %shard_map.93 = (bf16[512,768]{1,0:T(8,128)(2,1)}, bf16[512,1024]{1,0:T(8,128)(2,1)}, bf16[512,1024]{1,0:T(8,128)(2,1)}, bf16[512,1024]{1,0:T(8,128)(2,1)}) custom-call(bf16[512,1024]{1,0:T(8,128)(2,1)} %q_ref.1, bf16[512,1024]{1,0:T(8,128)(2,1)} %k_ref.1, bf16[512,1024]{1,0:T(8,128)(2,1)} %v_ref.1, f32[1,1024]{1,0:T(1,128)} %bitcast.1, ...), custom_call_target="tpu_custom_call" | custom-call | flops 12000000000 | bytes 10000000 | tf_op jit(solution)/shard_map/pallas_call | solution.py:415
  125.5 0.0 copy-start.2
  125.5 0.0 copy-start.1
  125.5 2.2 %copy.14 = bf16[512,768]{1,0:T(8,128)(2,1)} copy(bf16[512,768]{1,0:T(8,128)(2,1)} %get-tuple-element.8) | data formatting | bytes 1572864
  127.7 0.0 copy-done.2
  127.7 1.0 copy.15
  128.7 0.0 copy-done.1
  128.7 0.0 copy-start
  128.7 1.0 copy.16
  129.6 0.6 copy-done
  130.3 1.0 copy.17
Async XLA Ops:
  125.5 2.2 %copy-start.2 = (bf16[512,1024]{1,0:T(8,128)(2,1)S(1)}, bf16[512,1024]{1,0:T(8,128)(2,1)}, u32[]{:S(2)}) copy-start(bf16[512,1024]{1,0:T(8,128)(2,1)} %get-tuple-element.9) | copy-start | bytes 3145732
  125.5 3.2 %copy-start.1 = (bf16[512,1024]{1,0:T(8,128)(2,1)S(1)}, bf16[512,1024]{1,0:T(8,128)(2,1)}, u32[]{:S(2)}) copy-start(bf16[512,1024]{1,0:T(8,128)(2,1)} %get-tuple-element.10) | copy-start | bytes 3145732
  128.7 1.6 %copy-start = (bf16[512,1024]{1,0:T(8,128)(2,1)S(1)}, bf16[512,1024]{1,0:T(8,128)(2,1)}, u32[]{:S(2)}) copy-start(bf16[512,1024]{1,0:T(8,128)(2,1)} %get-tuple-element.11) | copy-start | bytes 3145732

commit v2 on v1

--- a/solution.py
+++ b/solution.py
@@ -110,14 +110,16 @@
     q_ref, k_ref, v_ref, gain_ref, w_ref, og_ref,
     mixed_ref, dq_ref, dk_ref, dv_ref,
     wall, ogall, att, gh, scores, hid, dout,
-    pacc, csend, cin, xsend, xin, sbuf, pbuf, psend, rbuf, gbuf, gsend,
+    macc, csend, cin, xsend, xin, sbuf, pbuf, psend, rbuf, gbuf, gsend,
     local_sem, up_sem, down_sem, z_sem, ysend_sem, yrecv_sem, ogsend_sem, ogrecv_sem,
     psend_sem, precv_sem, rsend_sem, rrecv_sem, csend_sem, crecv_sem, xsend_sem, xrecv_sem,
 ):
     rows = q_ref.shape[0]
     heads = q_ref.shape[1] // HD
-    half_cols = wall.shape[3]
+    half_cols = w_ref.shape[1] // 2
     piece = half_cols // PIECES
+    band = wall.shape[2]
+    mid = heads // 2
     part = heads // SPANS
     g = lax.axis_index("groups")
     z = lax.axis_index("ctx")
@@ -148,28 +150,32 @@
     pl.semaphore_wait(barrier, 3 + jnp.where(z < last, 1, 0) + jnp.where(z > 0, 1, 0))
 
     def cols(index, width):
+        if isinstance(index, int):
+            return slice(index * width, (index + 1) * width)
         return pl.ds(pl.multiple_of(index * width, HD), width)
 
     def head_cols(index):
         return cols(index, HD)
 
-    def w_piece(k, half, j):
-        return wall.at[k, half, :, cols(j, piece)]
-
-    def own_piece(j):
-        return w_ref.at[:, cols(g * PIECES + j, piece)]
-
-    def z_copy(src, k, j, send, to):
-        return remote(src, w_piece(k, g, j), send.at[k, j], z_sem.at[k, j], to)
-
-    def up_copy(k, j, src=None):
-        return z_copy(w_piece(k, g, j) if src is None else src, k, j, up_sem, to_up)
-
-    def down_copy(k, j, src=None):
-        return z_copy(w_piece(k, g, j) if src is None else src, k, j, down_sem, to_down)
-
-    def y_copy(k, half, j):
-        return remote(w_piece(k, half, j), w_piece(k, half, j), ysend_sem.at[k, j], yrecv_sem.at[k, j], to_y)
+    def w_piece(k, b, half, j):
+        return wall.at[k, b, :, cols(half * PIECES + j, piece)]
+
+    def own_piece(b, j):
+        return w_ref.at[b * band:(b + 1) * band, cols(g * PIECES + j, piece)]
+
+    def z_copy(src, k, b, j, send, to):
+        return remote(src, w_piece(k, b, g, j), send.at[k, b, j], z_sem.at[k, b, j], to)
+
+    def up_copy(k, b, j, src=None):
+        return z_copy(w_piece(k, b, g, j) if src is None else src, k, b, j, up_sem, to_up)
+
+    def down_copy(k, b, j, src=None):
+        return z_copy(w_piece(k, b, g, j) if src is None else src, k, b, j, down_sem, to_down)
+
+    def y_copy(k, b, half, j):
+        return remote(
+            w_piece(k, b, half, j), w_piece(k, b, half, j), ysend_sem.at[k, b, j], yrecv_sem.at[k, b, j], to_y
+        )
 
     def og_copy(slot, index, src, to):
         return remote(src, ogall.at[slot], ogsend_sem.at[index], ogrecv_sem.at[index], to)
@@ -180,13 +186,20 @@
     og_forward = og_copy(across, 2, ogall.at[across], to_core)
     own_og = pltpu.make_async_copy(og_ref, ogall.at[h], local_sem.at[2])
     own_w = [
-        pltpu.make_async_copy(w_ref.at[:, i * half_cols:(i + 1) * half_cols], wall.at[z, i], local_sem.at[i])
+        pltpu.make_async_copy(w_ref.at[i * band:(i + 1) * band], wall.at[z, i], local_sem.at[i])
         for i in range(2)
     ]
 
-    for j in range(PIECES):
-        pl.when(z < last)(lambda j=j: up_copy(z, j, own_piece(j)).start())
-        pl.when(z > 0)(lambda j=j: down_copy(z, j, own_piece(j)).start())
+    def send_own(b):
+        for j in range(PIECES):
+            pl.when(z < last)(lambda j=j: up_copy(z, b, j, own_piece(b, j)).start())
+            pl.when(z > 0)(lambda j=j: down_copy(z, b, j, own_piece(b, j)).start())
+
+    def for_heads(low, high, step):
+        for i in range(low, high):
+            step(i)
+
+    send_own(0)
     og_x.start()
     og_core.start()
     own_og.start()
@@ -202,11 +215,10 @@
     def r_copy(i, src):
         return remote(span(src, i), span(gbuf, i), rsend_sem.at[i], rrecv_sem.at[i], to_down)
 
-    def state_step(i, carry):
+    def state_step(i):
         sbuf[i] = mul(k_ref[:, head_cols(i)], v_ref[:, head_cols(i)], TN).astype(BF16)
-        return carry
-
-    lax.fori_loop(0, heads, state_step, 0)
+
+    for_heads(0, heads, state_step)
 
     @pl.when(z == 0)
     def _():
@@ -214,35 +226,47 @@
             p_copy(i, sbuf).start()
         pbuf[...] = jnp.zeros_like(pbuf)
 
-    causal = lax.broadcasted_iota(jnp.int32, (rows, rows), 0) >= lax.broadcasted_iota(jnp.int32, (rows, rows), 1)
-
-    def score_step(i, carry):
-        own = jnp.where(causal, mul(q_ref[:, head_cols(i)], k_ref[:, head_cols(i)], NT), 0.0).astype(BF16)
-        scores[i] = own
-        att[:, head_cols(i)] = mul(own, v_ref[:, head_cols(i)], NN)
-        return carry
-
-    lax.fori_loop(0, heads, score_step, 0)
-
-    def pass_on(s):
+    block = rows // 2
+    causal = lax.broadcasted_iota(jnp.int32, (block, block), 0) >= lax.broadcasted_iota(jnp.int32, (block, block), 1)
+    early, late = slice(0, block), slice(block, rows)
+
+    def masked(left, right):
+        first = jnp.where(causal, mul(left[:block], right[:block], NT), 0.0).astype(BF16)
+        cross = mul(left[block:], right[:block], NT).astype(BF16)
+        second = jnp.where(causal, mul(left[block:], right[block:], NT), 0.0).astype(BF16)
+        return first, jnp.concatenate([cross, second], axis=1)
+
+    def score_step(i):
+        at = head_cols(i)
+        first, below = masked(q_ref[:, at], k_ref[:, at])
+        scores[i, early, early] = first
+        scores[i, late, :] = below
+        att[early, at] = mul(first, v_ref[early, at], NN)
+        att[late, at] = mul(below, v_ref[:, at], NN)
+
+    def pass_on(b, s):
         for j in range(PIECES):
-            @pl.when((s > 0) & (z - s >= 0))
+            @pl.when(z - s >= 0)
             def _():
                 k = z - s
-                up_copy(k, j).wait_recv()
-                y_copy(k, g, j).start()
-                pl.when(z < last)(lambda: up_copy(k, j).start())
-
-            @pl.when((s > 0) & (z + s <= last))
+                up_copy(k, b, j).wait_recv()
+                y_copy(k, b, g, j).start()
+                pl.when(z < last)(lambda: up_copy(k, b, j).start())
+
+            @pl.when(z + s <= last)
             def _():
                 k = z + s
-                down_copy(k, j).wait_recv()
-                y_copy(k, g, j).start()
-                pl.when(z > 0)(lambda: down_copy(k, j).start())
-
+                down_copy(k, b, j).wait_recv()
+                y_copy(k, b, g, j).start()
+                pl.when(z > 0)(lambda: down_copy(k, b, j).start())
+
+    for_heads(0, mid, score_step)
+    pass_on(0, 1)
+    for_heads(mid, heads, score_step)
     og_copy(across, 1, og_ref, to_x).wait_recv()
     og_forward.start()
-    pass_on(1)
+    pass_on(0, 2)
+    send_own(1)
 
     @pl.when(z > 0)
     def _():
@@ -255,82 +279,77 @@
                 psend[at] = (sbuf[at].astype(F32) + pbuf[at].astype(F32)).astype(BF16)
                 p_copy(i, psend).start()
 
-    def hidden_step(i, carry):
+    def hidden_step(i):
         at = head_cols(i)
         whole = att[:, at] + mul(q_ref[:, at], pbuf[i], NN)
         att[:, at] = whole
         scale = lax.rsqrt(jnp.mean(whole * whole, axis=-1, keepdims=True) + 1e-06)
         hid[:, at] = (whole * scale * gain_ref[:, at]).astype(BF16)
-        return carry
-
-    lax.fori_loop(0, heads, hidden_step, 0)
+
+    for_heads(0, heads, hidden_step)
 
     own_og.wait()
     for copy in own_w:
         copy.wait()
     og_core.wait_recv()
     og_forward.wait_recv()
-    gh[...] = jnp.zeros_like(gh)
-
-    def core_copy(xk, half):
-        return remote(csend.at[xk, half], cin.at[xk, half], csend_sem.at[xk, half], crecv_sem.at[xk, half], to_core)
-
-    def x_copy(half):
-        return remote(xsend.at[half], xin.at[half], xsend_sem.at[half], xrecv_sem.at[half], to_x)
-
-    def work(k, half):
+
+    def core_copy(xk):
+        return remote(csend.at[xk], cin.at[xk], csend_sem.at[xk], crecv_sem.at[xk], to_core)
+
+    x_copy = remote(xsend, xin, xsend_sem.at[0], xrecv_sem.at[0], to_x)
+
+    def work(k, b, opening):
+        lanes = slice(b * band, (b + 1) * band)
         xk, ck = k // 2, k % 2
-        weight = wall[k, half]
-        term = mul(hid[...], weight, NN)
-
-        @pl.when(ck != c)
-        def _():
-            csend[xk, half] = term.astype(BF16)
-            core_copy(xk, half).start()
-
-        @pl.when(ck == c)
-        def _():
-            pacc[xk, half] = term
-
-        gh[...] += mul(ogall[k, :, cols(half, half_cols)], weight, NT)
-
-        @pl.when(ck == c)
-        def _():
-            core_copy(xk, half).wait_recv()
-            both = pacc[xk, half] + cin[xk, half].astype(F32)
-
-            @pl.when(xk == x)
-            def _():
-                pacc[xk, half] = both
-
-            @pl.when(xk != x)
-            def _():
-                xsend[half] = both.astype(BF16)
-                x_copy(half).start()
-
-    def ring_step(s, carry):
-        pl.when(s > 1)(lambda: pass_on(s))
-
-        def sub_step(i, inner):
-            above, late = i % 2, i // 2
-            k = jnp.where(above == 0, z - s, z + s)
-            half = jnp.where(late == 0, g, 1 - g)
-
-            @pl.when((k >= 0) & (k <= last) & ((s > 0) | (above == 0)))
-            def _():
-                @pl.when((late == 1) & (s > 0))
+        weight = wall[k, b]
+        term = mul(hid[:, lanes], weight, NN)
+        if b == 0:
+            macc[k] = term
+        else:
+            term = macc[k] + term
+
+            @pl.when(ck != c)
+            def _():
+                csend[xk] = term.astype(BF16)
+                core_copy(xk).start()
+
+            @pl.when(ck == c)
+            def _():
+                macc[k] = term
+
+        back = mul(ogall[k], weight, NT)
+        gh[:, lanes] = back if opening else gh[:, lanes] + back
+        if b == 1:
+            @pl.when(ck == c)
+            def _():
+                core_copy(xk).wait_recv()
+                both = macc[k] + cin[xk].astype(F32)
+
+                @pl.when(xk == x)
                 def _():
-                    for j in range(PIECES):
-                        y_copy(k, half, j).wait_recv()
-                work(k, half)
-            return inner
-
-        lax.fori_loop(0, 4, sub_step, 0)
-        return carry
-
-    lax.fori_loop(0, 4, ring_step, 0)
-
-    def norm_step(i, carry):
+                    macc[k] = both
+
+                @pl.when(xk != x)
+                def _():
+                    xsend[...] = both.astype(BF16)
+                    x_copy.start()
+
+    def ring(b, low, high):
+        def sub_step(i, carry):
+            s = i // 2
+            k = jnp.where(i % 2 == 0, z - s, z + s)
+
+            @pl.when((k >= 0) & (k <= last))
+            def _():
+                for j in range(PIECES):
+                    y_copy(k, b, 1 - g, j).wait_recv()
+                work(k, b, False)
+            return carry
+
+        lax.fori_loop(2 * low, 2 * high, sub_step, 0)
+
+    def norm_step(i):
         at = head_cols(i)
         whole = att[:, at]
         scale = lax.rsqrt(jnp.mean(whole * whole, axis=-1, keepdims=True) + 1e-06)
@@ -339,74 +358,95 @@
         grad = ((scaled - whole * inner) * scale).astype(BF16)
         dout[:, at] = grad
         rbuf[i] = mul(q_ref[:, at], grad, TN).astype(BF16)
-        return carry
-
-    lax.fori_loop(0, heads, norm_step, 0)
-
-    @pl.when(z == last)
-    def _():
-        for i in range(SPANS):
-            r_copy(i, rbuf).start()
-        gbuf[...] = jnp.zeros_like(gbuf)
-
-    def grad_step(i, carry):
+
+    def grad_step(i):
         at = head_cols(i)
         grad = dout[:, at]
-        back = jnp.where(causal, mul(grad, v_ref[:, at], NT), 0.0).astype(BF16)
-        dq_ref[:, at] = (mul(back, k_ref[:, at], NN) + mul(grad, pbuf[i], NT)).astype(BF16)
-        att[:, at] = mul(back, q_ref[:, at], TN)
-        gh[:, at] = mul(scores[i], grad, TN)
-        return carry
-
-    lax.fori_loop(0, heads, grad_step, 0)
-
-    @pl.when(z < last)
-    def _():
-        for i in range(SPANS):
-            r_copy(i, gsend).wait_recv()
-
-            @pl.when(z > 0)
-            def _():
-                at = pl.ds(i * part, part)
-                gsend[at] = (rbuf[at].astype(F32) + gbuf[at].astype(F32)).astype(BF16)
-                r_copy(i, gsend).start()
-
-    def last_step(i, carry):
+        first, below = masked(grad, v_ref[:, at])
+        outer = mul(grad, pbuf[i], NT)
+        dq_ref[early, at] = (mul(first, k_ref[early, at], NN) + outer[:block]).astype(BF16)
+        dq_ref[late, at] = (mul(below, k_ref[:, at], NN) + outer[block:]).astype(BF16)
+        query = q_ref[:, at]
+        kept = mul(below, query[block:], TN)
+        att[early, at] = kept[:block] + mul(first, query[:block], TN)
+        att[late, at] = kept[block:]
+        given = mul(scores[i, late, :], grad[block:], TN)
+        gh[early, at] = given[:block] + mul(scores[i, early, early], grad[:block], TN)
+        gh[late, at] = given[block:]
+
+    def suffix_start(low, high):
+        @pl.when(z == last)
+        def _():
+            for i in range(low, high):
+                r_copy(i, rbuf).start()
+
+    def suffix_pass(low, high):
+        @pl.when(z < last)
+        def _():
+            for i in range(low, high):
+                r_copy(i, gsend).wait_recv()
+
+                @pl.when(z > 0)
+                def _():
+                    at = pl.ds(i * part, part)
+                    gsend[at] = (rbuf[at].astype(F32) + gbuf[at].astype(F32)).astype(BF16)
+                    r_copy(i, gsend).start()
+
+    def last_step(i):
         at = head_cols(i)
         dk_ref[:, at] = (att[:, at] + mul(v_ref[:, at], gbuf[i], NT)).astype(BF16)
         dv_ref[:, at] = (gh[:, at] + mul(k_ref[:, at], gbuf[i], NN)).astype(BF16)
-        return carry
-
-    lax.fori_loop(0, heads, last_step, 0)
-
-    for half in range(2):
-        x_copy(half).wait_recv()
-        mixed_ref[:, half * half_cols:(half + 1) * half_cols] = (
-            pacc[x, half] + xin[half].astype(F32)
-        ).astype(BF16)
+
+    @pl.when(z == last)
+    def _():
+        gbuf[...] = jnp.zeros_like(gbuf)
+
+    work(z, 0, True)
+    ring(0, 1, 3)
+    pass_on(0, 3)
+    ring(0, 3, 4)
+    pass_on(1, 1)
+    for_heads(0, mid, norm_step)
+    suffix_start(0, SPANS // 2)
+    pass_on(1, 2)
+    for_heads(0, mid, grad_step)
+    work(z, 1, True)
+    ring(1, 1, 2)
+    pass_on(1, 3)
+    ring(1, 2, 3)
+    suffix_pass(0, SPANS // 2)
+    ring(1, 3, 4)
+    for_heads(mid, heads, norm_step)
+    suffix_start(SPANS // 2, SPANS)
+    for_heads(0, mid, last_step)
+    for_heads(mid, heads, grad_step)
+    suffix_pass(SPANS // 2, SPANS)
+    for_heads(mid, heads, last_step)
+
+    x_copy.wait_recv()
+    mixed_ref[...] = (macc[h] + xin[...].astype(F32)).astype(BF16)
 
     og_core.wait_send()
     og_x.wait_send()
     og_forward.wait_send()
-    for half in range(2):
-        x_copy(half).wait_send()
-        for xk in range(2):
-            core_copy(xk, half).wait_send()
+    x_copy.wait_send()
+    for xk in range(2):
+        core_copy(xk).wait_send()
     for i in range(SPANS):
         pl.when(z < last)(lambda i=i: p_copy(i, sbuf).wait_send())
         pl.when(z > 0)(lambda i=i: r_copy(i, rbuf).wait_send())
     for k in range(4):
-        for j in range(PIECES):
-            pl.when((z >= k) & (z < last))(lambda k=k, j=j: up_copy(k, j).wait_send())
-            pl.when((z <= k) & (z > 0))(lambda k=k, j=j: down_copy(k, j).wait_send())
-            pl.when(z != k)(lambda k=k, j=j: y_copy(k, g, j).wait_send())
+        for b in range(2):
+            for j in range(PIECES):
+                pl.when((z >= k) & (z < last))(lambda: up_copy(k, b, j).wait_send())
+                pl.when((z <= k) & (z > 0))(lambda: down_copy(k, b, j).wait_send())
+                pl.when(z != k)(lambda: y_copy(k, b, g, j).wait_send())
 
 
 def on_device_fused(queries, key_rows, value_rows, norm_gain, out_weight, out_grad):
     rows, width = queries.shape
     heads = width // HD
     share = out_weight.shape[1]
-    half = share // 2
     inside = pl.BlockSpec(memory_space=pltpu.VMEM)
     anywhere = pl.BlockSpec(memory_space=pl.ANY)
     grid_of = jax.ShapeDtypeStruct((rows, width), BF16)
@@ -418,24 +458,24 @@
         in_specs=[inside] * 4 + [anywhere] * 2,
         out_specs=(inside,) * 4,
         scratch_shapes=[
-            pltpu.VMEM((4, 2, width, half), BF16),
+            pltpu.VMEM((4, 2, width // 2, share), BF16),
             pltpu.VMEM((4, rows, share), BF16),
             pltpu.VMEM((rows, width), F32),
             pltpu.VMEM((rows, width), F32),
             pltpu.VMEM((heads, rows, rows), BF16),
             pltpu.VMEM((rows, width), BF16),
             pltpu.VMEM((rows, width), BF16),
-            pltpu.VMEM((2, 2, rows, half), F32),
-            pltpu.VMEM((2, 2, rows, half), BF16),
-            pltpu.VMEM((2, 2, rows, half), BF16),
-            pltpu.VMEM((2, rows, half), BF16),
-            pltpu.VMEM((2, rows, half), BF16),
+            pltpu.VMEM((4, rows, share), F32),
+            pltpu.VMEM((2, rows, share), BF16),
+            pltpu.VMEM((2, rows, share), BF16),
+            pltpu.VMEM((rows, share), BF16),
+            pltpu.VMEM((rows, share), BF16),
             states, states, states, states, states, states,
             dma((3,)),
-            dma((4, PIECES)), dma((4, PIECES)), dma((4, PIECES)), dma((4, PIECES)), dma((4, PIECES)),
+            dma((4, 2, PIECES)), dma((4, 2, PIECES)), dma((4, 2, PIECES)), dma((4, 2, PIECES)), dma((4, 2, PIECES)),
             dma((3,)), dma((3,)),
             dma((SPANS,)), dma((SPANS,)), dma((SPANS,)), dma((SPANS,)),
-            dma((2, 2)), dma((2, 2)), dma((2,)), dma((2,)),
+            dma((2,)), dma((2,)), dma((1,)), dma((1,)),
         ],
         compiler_params=pltpu.CompilerParams(
             collective_id=0, has_side_effects=True, vmem_limit_bytes=56 * 1024 * 1024

time: 131 us -> 110 us (0.84)
  Pallas kernels: 125 us -> 104 us
    pallas_call x1, Pallas kernels: 125 us -> 104 us  [on_device_fused(): pl.pallas_call(fused_kernel, out_shape=(jax.ShapeDtypeStruct((rows, share...]
where the time goes in v2:
time: 110 us
  Pallas kernels  104 us (95%)
  local copies, waits for them, and re-layouts  5.76 us (5%)
    pallas_call x1, Pallas kernels, on_device_fused(): pl.pallas_call(fused_kernel, out_shape=(jax.ShapeDtypeStruct((rows, share...  104 us
    unnamed x10, local copies, waits for them, and re-layouts  5.76 us

profile of v2, /device:TPU:0, one launch (start us, length us, event | category | flops | bytes accessed | tf_op | source)
XLA Modules:
  0.0 110.1 jit_solution(3994110693532646163)
XLA Ops:
  0.6 103.7 %shard_map.93 = (bf16[512,768]{1,0:T(8,128)(2,1)}, bf16[512,1024]{1,0:T(8,128)(2,1)}, bf16[512,1024]{1,0:T(8,128)(2,1)}, bf16[512,1024]{1,0:T(8,128)(2,1)}) custom-call(bf16[512,1024]{1,0:T(8,128)(2,1)} %q_ref.1, bf16[512,1024]{1,0:T(8,128)(2,1)} %k_ref.1, bf16[512,1024]{1,0:T(8,128)(2,1)} %v_ref.1, f32[1,1024]{1,0:T(1,128)} %bitcast.1, ...), custom_call_target="tpu_custom_call" | custom-call | flops 12000000000 | bytes 10000000 | tf_op jit(solution)/shard_map/pallas_call | solution.py:455
  104.3 0.0 copy-start.2
  104.3 0.0 copy-start.1
  104.3 2.2 %copy.14 = bf16[512,768]{1,0:T(8,128)(2,1)} copy(bf16[512,768]{1,0:T(8,128)(2,1)} %get-tuple-element.8) | data formatting | bytes 1572864
  106.5 0.0 copy-done.2
  106.5 1.0 copy.15
  107.5 0.0 copy-done.1
  107.5 0.0 copy-start
  107.5 1.0 copy.16
  108.5 0.6 copy-done
  109.1 1.0 copy.17
Async XLA Ops:
  104.3 2.2 %copy-start.2 = (bf16[512,1024]{1,0:T(8,128)(2,1)S(1)}, bf16[512,1024]{1,0:T(8,128)(2,1)}, u32[]{:S(2)}) copy-start(bf16[512,1024]{1,0:T(8,128)(2,1)} %get-tuple-element.9) | copy-start | bytes 3145732
  104.3 3.2 %copy-start.1 = (bf16[512,1024]{1,0:T(8,128)(2,1)S(1)}, bf16[512,1024]{1,0:T(8,128)(2,1)}, u32[]{:S(2)}) copy-start(bf16[512,1024]{1,0:T(8,128)(2,1)} %get-tuple-element.10) | copy-start | bytes 3145732
  107.5 1.6 %copy-start = (bf16[512,1024]{1,0:T(8,128)(2,1)S(1)}, bf16[512,1024]{1,0:T(8,128)(2,1)}, u32[]{:S(2)}) copy-start(bf16[512,1024]{1,0:T(8,128)(2,1)} %get-tuple-element.11) | copy-start | bytes 3145732

commit v3 on v2

--- a/solution.py
+++ b/solution.py
@@ -266,7 +266,6 @@
     og_copy(across, 1, og_ref, to_x).wait_recv()
     og_forward.start()
     pass_on(0, 2)
-    send_own(1)
 
     @pl.when(z > 0)
     def _():
@@ -278,6 +277,8 @@
                 at = pl.ds(i * part, part)
                 psend[at] = (sbuf[at].astype(F32) + pbuf[at].astype(F32)).astype(BF16)
                 p_copy(i, psend).start()
+
+    send_own(1)
 
     def hidden_step(i):
         at = head_cols(i)

time: 110 us -> 102 us (0.927)
  Pallas kernels: 104 us -> 95.3 us
    pallas_call x1, Pallas kernels: 104 us -> 95.3 us  [on_device_fused(): pl.pallas_call(fused_kernel, out_shape=(jax.ShapeDtypeStruct((rows, share...]
where the time goes in v3:
time: 102 us
  Pallas kernels  95.3 us (93%)
  local copies, waits for them, and re-layouts  5.76 us (6%)
    pallas_call x1, Pallas kernels, on_device_fused(): pl.pallas_call(fused_kernel, out_shape=(jax.ShapeDtypeStruct((rows, share...  95.3 us
    unnamed x10, local copies, waits for them, and re-layouts  5.76 us

profile of v3, /device:TPU:0, one launch (start us, length us, event | category | flops | bytes accessed | tf_op | source)
XLA Modules:
  0.0 101.7 jit_solution(16513473573994484658)
XLA Ops:
  0.6 95.3 %shard_map.93 = (bf16[512,768]{1,0:T(8,128)(2,1)}, bf16[512,1024]{1,0:T(8,128)(2,1)}, bf16[512,1024]{1,0:T(8,128)(2,1)}, bf16[512,1024]{1,0:T(8,128)(2,1)}) custom-call(bf16[512,1024]{1,0:T(8,128)(2,1)} %q_ref.1, bf16[512,1024]{1,0:T(8,128)(2,1)} %k_ref.1, bf16[512,1024]{1,0:T(8,128)(2,1)} %v_ref.1, f32[1,1024]{1,0:T(1,128)} %bitcast.1, ...), custom_call_target="tpu_custom_call" | custom-call | flops 12000000000 | bytes 10000000 | tf_op jit(solution)/shard_map/pallas_call | solution.py:456
  95.9 0.0 copy-start.2
  95.9 0.0 copy-start.1
  95.9 2.2 %copy.14 = bf16[512,768]{1,0:T(8,128)(2,1)} copy(bf16[512,768]{1,0:T(8,128)(2,1)} %get-tuple-element.8) | data formatting | bytes 1572864
  98.1 0.0 copy-done.2
  98.1 1.0 copy.15
  99.1 0.0 copy-done.1
  99.1 0.0 copy-start
  99.1 1.0 copy.16
  100.1 0.6 copy-done
  100.7 1.0 copy.17
Async XLA Ops:
  95.9 2.2 %copy-start.2 = (bf16[512,1024]{1,0:T(8,128)(2,1)S(1)}, bf16[512,1024]{1,0:T(8,128)(2,1)}, u32[]{:S(2)}) copy-start(bf16[512,1024]{1,0:T(8,128)(2,1)} %get-tuple-element.9) | copy-start | bytes 3145732
  95.9 3.2 %copy-start.1 = (bf16[512,1024]{1,0:T(8,128)(2,1)S(1)}, bf16[512,1024]{1,0:T(8,128)(2,1)}, u32[]{:S(2)}) copy-start(bf16[512,1024]{1,0:T(8,128)(2,1)} %get-tuple-element.10) | copy-start | bytes 3145732
  99.1 1.6 %copy-start = (bf16[512,1024]{1,0:T(8,128)(2,1)S(1)}, bf16[512,1024]{1,0:T(8,128)(2,1)}, u32[]{:S(2)}) copy-start(bf16[512,1024]{1,0:T(8,128)(2,1)} %get-tuple-element.11) | copy-start | bytes 3145732
